TPU v7x, 512 devices: a whole 4x4x16 slice. The times are simulated.
512 devices in a mesh: canal: 64 (over z, y), cross: 8 (over x, core).
Axes of the slice: x: 4, y: 4, z: 16, core: 2. Of those that a mesh axis runs over, the one named last changes fastest.
Arguments:
- conserved: float32 [128, 7, 128, 256], P('canal', None, 'cross'), may hold values from -24 to 24
- iblank: int32 [128, 128, 256], P('canal', 'cross'), may hold values from 0 to 2, as said below
- step_scale: float32 [128, 128, 256], P('canal', 'cross'), may hold values from 0.25 to 8
- speeds: float32 [3, 7], replicated, may hold values from -2 to 2
- left_vectors: float32 [7, 7], replicated, may hold values from -2 to 2
- right_vectors: float32 [7, 7], replicated, may hold values from -2 to 2
Outputs:
- update: float32 [128, 7, 128, 256], P('canal', None, 'cross')
Inputs may be any that keep to these rules, and one draw needn't show every extreme that they name: iblank is 0 at hole cells inside the hulls, 2 at fringe cells around them and 1 elsewhere.
All inputs are finite; a program needn't handle non-finite values.
Results may differ from a plain program's by a relative error of at most 0.00012.
Values sent between devices are 32-bit elements; how exact they have to be, the bound alone decides.
A program may use at most 64 MiB of HBM per device.

v0:
```python
import functools

import jax
import jax.numpy as jnp
from jax import lax
from jax.experimental import pallas as pl
from jax.experimental.pallas import tpu as pltpu
from jax.sharding import PartitionSpec as P

MESH = pl.DeviceIdType.MESH
F32 = jnp.float32
NVAR = 7
TILE = (8, 128)


def partner_of(pair, crosses):
    place = pair // crosses
    rest = lax.rem(pair, crosses)
    if crosses == 8:
        group = 4 * (rest // 4) + lax.rem(lax.rem(rest, 4) + place, 4)
    else:
        group = rest
    return group, place


def pair_of(group, place, crosses):
    if crosses == 8:
        return 8 * place + 4 * (group // 4) + lax.rem(lax.rem(group, 4) - place + 8, 4)
    return crosses * place + group


def factor(w, lower, centre, upper, p_one, q_one, p_two, q_two):
    damping = 0.25 * w
    reduced = w * (0.25 * p_two - lower)
    pivot = (1.0 + centre * w + damping * q_two) - reduced * p_one
    inverse = 1.0 / pivot
    q_new = -damping * inverse
    p_new = -(upper * w + reduced * q_one) * inverse
    return inverse, reduced * inverse, p_new, q_new


def join(swap, g_one, g_two, p_one, q_one, p_two, q_two):
    alpha = 1.0 - q_one * swap(q_two)
    beta = p_one - q_one * swap(p_two)
    gamma = g_one - q_one * swap(g_two)
    alpha_far, beta_far, gamma_far = swap(alpha), swap(beta), swap(gamma)
    return (gamma * alpha_far - beta * gamma_far) / (alpha * alpha_far - beta * beta_far)


def spread(speeds_ref, direction, index):
    forward = jnp.zeros(index.shape, F32)
    backward = jnp.zeros(index.shape, F32)
    for v in range(NVAR):
        speed = speeds_ref[direction, v]
        forward = jnp.where(index == v, jnp.maximum(speed, 0.0), forward)
        backward = jnp.where(index == v, jnp.maximum(-speed, 0.0), backward)
    return forward, backward


def coefficients(speeds_ref, direction, index, top):
    forward, backward = spread(speeds_ref, direction, index)
    lower = jnp.where(top, forward, backward) + 0.25
    upper = jnp.where(top, backward, forward) + 0.25
    return lower, 1.0 + forward + backward, upper


def kernel(
    canals,
    crosses,
    conserved,
    iblank,
    step_scale,
    speeds,
    left,
    right,
    update,
    known,
    weight,
    low_out,
    high_out,
    low_in,
    high_in,
    before,
    after,
    rows,
    send_one,
    recv_one,
    send_two,
    recv_two,
    turned,
    send_three,
    recv_three,
    vertical_weight,
    upright,
    v_inverse,
    v_multiplier,
    v_p,
    v_q,
    work_p,
    work_q,
    work_g,
    v_g,
    halo_send,
    halo_recv,
    send_sems,
    recv_sems,
):
    depth = 4 * canals
    block = min(depth, 128)
    blocks = depth // block
    places = canals // crosses
    half = canals // 2
    c = lax.axis_index("canal")
    k = lax.axis_index("cross")

    barrier = pltpu.get_barrier_semaphore()

    def greet_canal(i, carry):
        pl.semaphore_signal(
            barrier, inc=1, device_id=(lax.rem(c + i, canals), k), device_id_type=MESH
        )
        return carry

    def greet_cross(i, carry):
        pl.semaphore_signal(
            barrier, inc=1, device_id=(c, lax.rem(k + i, crosses)), device_id_type=MESH
        )
        return carry

    lax.fori_loop(1, canals, greet_canal, 0)
    lax.fori_loop(1, crosses, greet_cross, 0)

    for x in range(2):
        flag = iblank[x]
        live = (flag != 0).astype(F32)
        weight[x] = jnp.where(flag == 1, step_scale[x], 0.0)
        for v in range(NVAR):
            cells = conserved[x, v] * live
            known[x, v, 8:24, :] = cells
            low_out[x, v] = cells[0:2]
            high_out[x, v] = cells[14:16]

    pl.semaphore_wait(barrier, canals - 1 + crosses - 1)

    c_next, c_last = lax.rem(c + 1, canals), lax.rem(c + canals - 1, canals)
    k_next, k_last = lax.rem(k + 1, crosses), lax.rem(k + crosses - 1, crosses)
    own = known.at[:, :, pl.ds(8, 16), :]
    halo = []
    for number, (source, target, device) in enumerate(
        (
            (own, before, (c_next, k)),
            (own, after, (c_last, k)),
            (high_out, low_in, (c, k_next)),
            (low_out, high_in, (c, k_last)),
        )
    ):
        copy = pltpu.make_async_remote_copy(
            src_ref=source,
            dst_ref=target,
            send_sem=halo_send.at[number],
            recv_sem=halo_recv.at[number],
            device_id=device,
            device_id_type=MESH,
        )
        copy.start()
        halo.append(copy)

    lane = lax.broadcasted_iota(jnp.int32, TILE, 1)
    sub = lax.broadcasted_iota(jnp.int32, TILE, 0)
    upper_half = sub < 4

    def pack(matrices, target):
        for b in range(blocks):
            first = matrices[0][:, b * block : (b + 1) * block].T
            second = matrices[1][:, b * block : (b + 1) * block].T
            for n in range(block // 8):
                one, two = first[8 * n : 8 * n + 8], second[8 * n : 8 * n + 8]
                chunk = b * (block // 4) + 2 * n
                target[chunk] = jnp.where(upper_half, one, pltpu.roll(two, 4, 0))
                target[chunk + 1] = jnp.where(upper_half, pltpu.roll(one, 4, 0), two)

    pack([jnp.concatenate([weight[x]] * 8, axis=0) for x in range(2)], vertical_weight)
    v_top = lax.rem(sub, 4) == 0
    v_lower, v_centre, v_upper = coefficients(speeds, 2, lane // 16, v_top)

    def v_pick(ref, n, step):
        near, far = ref[n], ref[canals - 1 - n]
        if step:
            near = pltpu.roll(near, 8 - step, 0)
        if step != 2:
            far = pltpu.roll(far, (step + 6) % 8, 0)
        return jnp.where(v_top, near, far)

    def v_factor(n, carry):
        p_one, q_one, p_two, q_two = carry
        for step in range(4):
            w = v_pick(vertical_weight, n, step)
            inverse, multiplier, p_new, q_new = factor(
                w, v_lower, v_centre, v_upper, p_one, q_one, p_two, q_two
            )
            v_inverse[4 * n + step] = inverse
            v_multiplier[4 * n + step] = multiplier
            v_p[4 * n + step] = p_new
            v_q[4 * n + step] = q_new
            p_one, q_one, p_two, q_two = p_new, q_new, p_one, q_one
        return p_one, q_one, p_two, q_two

    zero = jnp.zeros(TILE, F32)
    lax.fori_loop(0, half, v_factor, (zero, zero, zero, zero))

    for copy in halo:
        copy.wait()

    has_last, has_next = c > 0, c < canals - 1
    low_mask, high_mask = k > 0, k < crosses - 1
    zi = lax.broadcasted_iota(jnp.int32, (16, depth), 1)
    for x in range(2):
        fluxes = []
        for v in range(NVAR):
            known[x, v, 6:8, :] = jnp.where(low_mask, low_in[x, v], 0.0)
            known[x, v, 24:26, :] = jnp.where(high_mask, high_in[x, v], 0.0)
            here = known[x, v, 8:24, :]
            if x == 0:
                minus_one = jnp.where(has_last, before[1, v], 0.0)
                minus_two = jnp.where(has_last, before[0, v], 0.0)
                plus_one = known[1, v, 8:24, :]
                plus_two = jnp.where(has_next, after[0, v], 0.0)
            else:
                minus_one = known[0, v, 8:24, :]
                minus_two = jnp.where(has_last, before[1, v], 0.0)
                plus_one = jnp.where(has_next, after[0, v], 0.0)
                plus_two = jnp.where(has_next, after[1, v], 0.0)
            canal_half = 0.5 * speeds[0, v]
            flux = (canal_half - 0.125) * plus_one - (canal_half + 0.125) * minus_one
            outer = plus_two + minus_two
            cross_half = 0.5 * speeds[1, v]
            flux += (cross_half - 0.125) * known[x, v, 9:25, :]
            flux -= (cross_half + 0.125) * known[x, v, 7:23, :]
            outer += known[x, v, 10:26, :] + known[x, v, 6:22, :]
            z_half = 0.5 * speeds[2, v]
            up_one = jnp.where(zi < depth - 1, pltpu.roll(here, depth - 1, 1), 0.0)
            up_two = jnp.where(zi < depth - 2, pltpu.roll(here, depth - 2, 1), 0.0)
            down_one = jnp.where(zi >= 1, pltpu.roll(here, 1, 1), 0.0)
            down_two = jnp.where(zi >= 2, pltpu.roll(here, 2, 1), 0.0)
            flux += (z_half - 0.125) * up_one - (z_half + 0.125) * down_one
            outer += up_two + down_two
            fluxes.append(flux + (outer + 18.0 * here) * (1.0 / 32.0))
        scale = weight[x]
        for v in range(NVAR):
            mixed = left[v, 0] * fluxes[0]
            for u in range(1, NVAR):
                mixed += left[v, u] * fluxes[u]
            rows[x, 16 * v : 16 * v + 16, :] = -(scale * mixed)
        rows[x, 112:128, :] = scale
    pack([rows[0], rows[1]], send_one)

    def send_tile(source, target, device, number):
        pltpu.make_async_remote_copy(
            src_ref=source,
            dst_ref=target,
            send_sem=send_sems.at[number],
            recv_sem=recv_sems.at[number],
            device_id=device,
            device_id_type=MESH,
        ).start()

    def wait_for(ref, count, sem):
        part = ref.at[pl.ds(0, count)]
        pltpu.make_async_copy(part, part, sem).wait()

    def send_canal(i, carry):
        for sign in (1, -1):
            other = lax.rem(c + sign * (half - i) + canals, canals)
            send_tile(send_one.at[other], recv_one.at[c], (other, k), 0)
        return carry

    opposite = lax.rem(c + half, canals)
    send_tile(send_one.at[opposite], recv_one.at[c], (opposite, k), 0)
    lax.fori_loop(1, half, send_canal, 0)
    pltpu.make_async_copy(send_one.at[c], recv_one.at[c], recv_sems.at[0]).start()
    wait_for(recv_one, canals, recv_sems.at[0])

    c_lower, c_centre, c_upper = coefficients(speeds, 0, lane // 16, upper_half)
    is_weight = lane >= 112

    def widen(tile):
        w = jnp.where(is_weight, tile, 0.0)
        w += pltpu.roll(w, 16, 1)
        w += pltpu.roll(w, 32, 1)
        return w + pltpu.roll(w, 64, 1)

    def c_forward(n, carry):
        g_one, p_one, q_one, g_two, p_two, q_two = carry
        near, far = recv_one[n], recv_one[canals - 1 - n]
        outer = jnp.where(upper_half, near, far)
        inner = pltpu.roll(jnp.where(upper_half, far, near), 4, 0)
        for step, source in enumerate((outer, inner)):
            w = widen(source)
            inverse, multiplier, p_new, q_new = factor(
                w, c_lower, c_centre, c_upper, p_one, q_one, p_two, q_two
            )
            g_new = (source * inverse - q_new * g_two) - multiplier * g_one
            work_g[2 * n + step] = g_new
            work_p[2 * n + step] = p_new
            work_q[2 * n + step] = q_new
            g_one, p_one, q_one, g_two, p_two, q_two = g_new, p_new, q_new, g_one, p_one, q_one
        return g_one, p_one, q_one, g_two, p_two, q_two

    g_one, p_one, q_one, g_two, p_two, q_two = lax.fori_loop(0, half, c_forward, (zero,) * 6)

    def c_swap(a):
        return pltpu.roll(a, 4, 0)

    x_one = join(c_swap, g_one, g_two, p_one, q_one, p_two, q_two)
    work_g[canals - 1] = x_one

    def c_back(i, carry):
        x_one, x_two = carry
        n = canals - 2 - i
        solved = (work_g[n] - work_q[n] * x_two) - work_p[n] * x_one
        work_g[n] = solved
        return solved, x_one

    lax.fori_loop(0, canals - 1, c_back, (x_one, c_swap(x_one)))

    def c_restore(n, carry):
        outer, inner = work_g[2 * n], pltpu.roll(work_g[2 * n + 1], 4, 0)
        for pair, tile in (
            (n, jnp.where(upper_half, outer, inner)),
            (canals - 1 - n, jnp.where(upper_half, inner, outer)),
        ):
            group, place = partner_of(pair, crosses)
            send_two[group * places + place] = jnp.where(is_weight, recv_one[pair], tile)
        return carry

    lax.fori_loop(0, half, c_restore, 0)

    def group_of(ref, position):
        return ref.at[pl.ds(position * places, places)]

    def send_cross(i, carry):
        other = lax.rem(k + i, crosses)
        send_tile(group_of(send_two, other), group_of(recv_two, k), (c, other), 1)
        return carry

    lax.fori_loop(1, crosses, send_cross, 0)
    pltpu.make_async_copy(group_of(send_two, k), group_of(recv_two, k), recv_sems.at[1]).start()
    wait_for(recv_two, canals, recv_sems.at[1])

    count = crosses // 2
    lines = 8 * places
    for pair in range(count):
        near = recv_two[pair * places : (pair + 1) * places].reshape(lines, 128)
        other = crosses - 1 - pair
        far = recv_two[other * places : (other + 1) * places].reshape(lines, 128)
        turned[pair] = jnp.concatenate([near, far], axis=0).T

    x_top = lane < lines
    x_lower, x_centre, x_upper = coefficients(speeds, 1, sub, x_top)

    def x_forward(pair, carry):
        g_one, p_one, q_one, g_two, p_two, q_two = carry
        for y in range(16):
            source = jnp.where(
                x_top,
                turned[pair, pl.ds(y, 8, stride=16), :],
                turned[pair, pl.ds(15 - y, 8, stride=16), :],
            )
            w = jnp.broadcast_to(source[7:8], TILE)
            inverse, multiplier, p_new, q_new = factor(
                w, x_lower, x_centre, x_upper, p_one, q_one, p_two, q_two
            )
            g_new = (source * inverse - q_new * g_two) - multiplier * g_one
            work_g[16 * pair + y] = g_new
            work_p[16 * pair + y] = p_new
            work_q[16 * pair + y] = q_new
            g_one, p_one, q_one, g_two, p_two, q_two = g_new, p_new, q_new, g_one, p_one, q_one
        return g_one, p_one, q_one, g_two, p_two, q_two

    g_one, p_one, q_one, g_two, p_two, q_two = lax.fori_loop(0, count, x_forward, (zero,) * 6)

    def x_swap(a):
        return pltpu.roll(a, lines, 1)

    x_one = join(x_swap, g_one, g_two, p_one, q_one, p_two, q_two)
    work_g[16 * count - 1] = x_one

    def x_back(i, carry):
        x_one, x_two = carry
        n = 16 * count - 2 - i
        solved = (work_g[n] - work_q[n] * x_two) - work_p[n] * x_one
        work_g[n] = solved
        return solved, x_one

    lax.fori_loop(0, 16 * count - 1, x_back, (x_one, x_swap(x_one)))

    for pair in range(count):
        for y in range(16):
            turned[pair, pl.ds(y, 8, stride=16), :] = jnp.where(
                x_top, work_g[16 * pair + y], work_g[16 * pair + 15 - y]
            )
        back = turned[pair].T
        send_three[pair * places : (pair + 1) * places] = back[:lines].reshape(places, 8, 128)
        other = crosses - 1 - pair
        send_three[other * places : (other + 1) * places] = back[lines:].reshape(places, 8, 128)

    def send_home(i, carry):
        place, other = i // crosses, lax.rem(i, crosses)
        place = lax.rem(place + c, places)
        other = lax.rem(other + k, crosses)
        target = pair_of(k, place, crosses)
        source = send_three.at[other * places + place]
        itself = jnp.logical_and(target == c, other == k)

        @pl.when(itself)
        def keep():
            pltpu.make_async_copy(source, recv_three.at[c], recv_sems.at[2]).start()

        @pl.when(jnp.logical_not(itself))
        def send():
            send_tile(source, recv_three.at[c], (target, other), 2)

        return carry

    lax.fori_loop(0, canals, send_home, 0)
    wait_for(recv_three, canals, recv_sems.at[2])

    def v_forward(n, carry):
        g_one, g_two = carry
        for step in range(4):
            i = 4 * n + step
            source = v_pick(recv_three, n, step)
            g_new = (source * v_inverse[i] - v_q[i] * g_two) - v_multiplier[i] * g_one
            v_g[i] = g_new
            g_one, g_two = g_new, g_one
        return g_one, g_two

    g_one, g_two = lax.fori_loop(0, half, v_forward, (zero, zero))

    def v_swap(a):
        return jnp.where(v_top, pltpu.roll(a, 7, 0), pltpu.roll(a, 1, 0))

    last = 2 * canals - 1
    x_one = join(v_swap, g_one, g_two, v_p[last], v_q[last], v_p[last - 1], v_q[last - 1])
    v_g[last] = x_one

    def v_back(i, carry):
        x_one, x_two = carry
        n = last - 1 - i
        solved = (v_g[n] - v_q[n] * x_two) - v_p[n] * x_one
        v_g[n] = solved
        return solved, x_one

    lax.fori_loop(0, last, v_back, (x_one, v_swap(x_one)))

    place_of = lax.rem(sub, 4)

    def v_restore(n, carry):
        near, far = [], []
        for part in range(2):
            base = 8 * n + 4 * part
            near_tile = v_g[base]
            far_tile = pltpu.roll(v_g[base], 2, 0)
            for step in range(1, 4):
                near_tile = jnp.where(
                    place_of == step, pltpu.roll(v_g[base + step], step, 0), near_tile
                )
                far_tile = jnp.where(
                    place_of == 3 - step,
                    pltpu.roll(v_g[base + step], (10 - step) % 8, 0),
                    far_tile,
                )
            near.append(near_tile)
            far.append(far_tile)
        far = far[::-1]
        at = pl.multiple_of(8 * n, 8)
        end = pl.multiple_of(depth - 8 - 8 * n, 8)
        for start, (one, two) in ((at, near), (end, far)):
            upright[0, pl.ds(start, 8), :] = jnp.where(upper_half, one, pltpu.roll(two, 4, 0))
            upright[1, pl.ds(start, 8), :] = jnp.where(upper_half, pltpu.roll(one, 4, 0), two)
        return carry

    lax.fori_loop(0, half // 2, v_restore, 0)

    for x in range(2):
        for b in range(blocks):
            third = upright[x, b * block : (b + 1) * block, :].T
            for v in range(NVAR):
                mixed = right[v, 0] * third[0:16]
                for u in range(1, NVAR):
                    mixed += right[v, u] * third[16 * u : 16 * u + 16]
                update[x, v, :, b * block : (b + 1) * block] = mixed

    wait_for(send_one, canals - 1, send_sems.at[0])
    wait_for(send_two, canals - places, send_sems.at[1])
    mine, unused = partner_of(c, crosses)

    @pl.when(mine == k)
    def sent_fewer():
        wait_for(send_three, canals - 1, send_sems.at[2])

    @pl.when(mine != k)
    def sent_all():
        wait_for(send_three, canals, send_sems.at[2])


def solution(mesh):
    canals, crosses = mesh.shape["canal"], mesh.shape["cross"]
    depth = 4 * canals
    cells = (2, NVAR, 16, depth)
    tiles = (canals,) + TILE

    def shards(conserved, iblank, step_scale, speeds, left_vectors, right_vectors):
        vmem = pl.BlockSpec(memory_space=pltpu.VMEM)
        smem = pl.BlockSpec(memory_space=pltpu.SMEM)

        def held(*shape):
            return pltpu.VMEM(shape, F32)

        return pl.pallas_call(
            functools.partial(kernel, canals, crosses),
            out_shape=jax.ShapeDtypeStruct(cells, F32),
            in_specs=[vmem, vmem, vmem, smem, smem, smem],
            out_specs=vmem,
            scratch_shapes=[
                held(2, NVAR, 32, depth),
                held(2, 16, depth),
                held(2, NVAR, 2, depth),
                held(2, NVAR, 2, depth),
                held(2, NVAR, 2, depth),
                held(2, NVAR, 2, depth),
                held(*cells),
                held(*cells),
                held(2, 128, depth),
                held(*tiles),
                held(*tiles),
                held(*tiles),
                held(*tiles),
                held(crosses // 2, 128, 16 * (canals // crosses)),
                held(*tiles),
                held(*tiles),
                held(*tiles),
                held(2, depth, 128),
                held(2 * canals, *TILE),
                held(2 * canals, *TILE),
                held(2 * canals, *TILE),
                held(2 * canals, *TILE),
                held(max(canals, 8 * crosses), *TILE),
                held(max(canals, 8 * crosses), *TILE),
                held(max(canals, 8 * crosses), *TILE),
                held(2 * canals, *TILE),
                pltpu.SemaphoreType.DMA((4,)),
                pltpu.SemaphoreType.DMA((4,)),
                pltpu.SemaphoreType.DMA((3,)),
                pltpu.SemaphoreType.DMA((3,)),
            ],
            compiler_params=pltpu.CompilerParams(
                collective_id=0, has_side_effects=True, vmem_limit_bytes=32 * 1024 * 1024
            ),
        )(conserved, iblank, step_scale, speeds, left_vectors, right_vectors)

    return jax.shard_map(
        shards,
        mesh=mesh,
        in_specs=(
            P("canal", None, "cross", None),
            P("canal", "cross", None),
            P("canal", "cross", None),
            P(),
            P(),
            P(),
        ),
        out_specs=P("canal", None, "cross", None),
        check_vma=False,
    )
```

profile of v0, /device:TPU:1, one launch (start us, length us, event | category | flops | bytes accessed | tf_op | source)
XLA Modules:
  0.0 83.0 jit_solution(5295385153478267618)
XLA Ops:
  0.0 0.0 copy-start
  0.0 0.9 %copy-done = f32[2,7,16,256]{3,2,1,0:T(8,128)S(1)} copy-done((f32[2,7,16,256]{3,2,1,0:T(8,128)S(1)}, f32[2,7,16,256]{3,2,1,0:T(8,128)}, u32[]{:S(2)}) %copy-start) | copy-done | bytes 229400
  0.9 0.0 copy-start.1
  0.9 0.8 copy-done.1
  1.7 0.0 copy-start.2
  1.7 0.8 copy-done.2
  2.5 0.0 copy-start.3
  2.5 0.7 copy-done.3
  3.1 0.0 copy-start.4
  3.1 0.7 copy-done.4
  3.8 0.0 copy-start.5
  3.8 0.7 copy-done.5
  4.5 77.8 %shard_map.64 = f32[2,7,16,256]{3,2,1,0:T(8,128)S(1)} custom-call(f32[2,7,16,256]{3,2,1,0:T(8,128)S(1)} %copy-done, s32[2,16,256]{2,1,0:T(8,128)S(1)} %copy-done.1, f32[2,16,256]{2,1,0:T(8,128)S(1)} %copy-done.2, f32[3,7]{1,0:T(4,128)S(1)} %copy-done.5, f32[7,7]{1,0:T(8,128)S(1)} %copy-done.3, f32[7,7]{1,0:T(8,128)S(1)} %copy-done.4), custom_call_target="tpu_custom_call" | custom-call | tf_op jit(solution)/shard_map/pallas_call | solution.py:520
  82.3 0.7 copy.8
Async XLA Ops:
  0.0 0.9 %copy-start = (f32[2,7,16,256]{3,2,1,0:T(8,128)S(1)}, f32[2,7,16,256]{3,2,1,0:T(8,128)}, u32[]{:S(2)}) copy-start(f32[2,7,16,256]{3,2,1,0:T(8,128)} %conserved.1) | copy-start | bytes 688132
  0.9 0.8 copy-start.1
  1.7 0.8 copy-start.2
  2.5 0.7 copy-start.3
  3.1 0.7 copy-start.4
  3.8 0.7 copy-start.5
where the time goes:
time: 83.4 us; the launch traced here: 83 us
  Pallas kernels  77.8 us (93%)
  local copies, waits for them, and re-layouts  5.2 us (6%)
    pallas_call x1, Pallas kernels, shards(): pl.pallas_call(functools.partial(kernel, canals, crosses), out_shape=jax....  77.8 us
    unnamed x13, local copies, waits for them, and re-layouts  5.2 us

commit v1 on v0

--- a/solution.py
+++ b/solution.py
@@ -13,20 +13,16 @@
 TILE = (8, 128)
 
 
-def partner_of(pair, crosses):
-    place = pair // crosses
-    rest = lax.rem(pair, crosses)
-    if crosses == 8:
-        group = 4 * (rest // 4) + lax.rem(lax.rem(rest, 4) + place, 4)
-    else:
-        group = rest
-    return group, place
-
-
-def pair_of(group, place, crosses):
-    if crosses == 8:
-        return 8 * place + 4 * (group // 4) + lax.rem(lax.rem(group, 4) - place + 8, 4)
-    return crosses * place + group
+def turn_of(canal, crosses):
+    return lax.rem(canal // 4, crosses)
+
+
+def partner_of(pair, canal, crosses):
+    return lax.rem(lax.rem(pair, crosses) + turn_of(canal, crosses), crosses), pair // crosses
+
+
+def pair_of(group, canal, place, crosses):
+    return crosses * place + lax.rem(group - turn_of(canal, crosses) + crosses, crosses)
 
 
 def factor(w, lower, centre, upper, p_one, q_one, p_two, q_two):
@@ -67,13 +63,19 @@
 def kernel(
     canals,
     crosses,
+    conserved_hbm,
+    iblank_hbm,
+    step_scale_hbm,
+    speeds_hbm,
+    left_hbm,
+    right_hbm,
+    update,
     conserved,
     iblank,
     step_scale,
     speeds,
     left,
     right,
-    update,
     known,
     weight,
     low_out,
@@ -100,10 +102,12 @@
     work_q,
     work_g,
     v_g,
+    load_sems,
     halo_send,
     halo_recv,
     send_sems,
     recv_sems,
+    entered,
 ):
     depth = 4 * canals
     block = min(depth, 128)
@@ -113,22 +117,42 @@
     c = lax.axis_index("canal")
     k = lax.axis_index("cross")
 
+    loads = [
+        pltpu.make_async_copy(source, target, load_sems.at[number])
+        for number, (source, target) in enumerate(
+            (
+                (iblank_hbm, iblank),
+                (conserved_hbm, conserved),
+                (step_scale_hbm, step_scale),
+                (speeds_hbm, speeds),
+                (left_hbm, left),
+                (right_hbm, right),
+            )
+        )
+    ]
+    for load in loads:
+        load.start()
+
     barrier = pltpu.get_barrier_semaphore()
-
-    def greet_canal(i, carry):
-        pl.semaphore_signal(
-            barrier, inc=1, device_id=(lax.rem(c + i, canals), k), device_id_type=MESH
-        )
-        return carry
-
-    def greet_cross(i, carry):
-        pl.semaphore_signal(
-            barrier, inc=1, device_id=(c, lax.rem(k + i, crosses)), device_id_type=MESH
-        )
-        return carry
-
-    lax.fori_loop(1, canals, greet_canal, 0)
-    lax.fori_loop(1, crosses, greet_cross, 0)
+    c_next, c_last = lax.rem(c + 1, canals), lax.rem(c + canals - 1, canals)
+    k_next, k_last = lax.rem(k + 1, crosses), lax.rem(k + crosses - 1, crosses)
+
+    def greet(device):
+        pl.semaphore_signal(barrier, inc=1, device_id=device, device_id_type=MESH)
+
+    def row_mate(i):
+        return 4 * (c // 4) + lax.rem(c + i, 4)
+
+    greet((c_next, k))
+    greet((c_last, k))
+    for i in range(1, canals // 4):
+        greet((lax.rem(c + 4 * i, canals), k))
+    for i in range(1, crosses):
+        greet((c, lax.rem(k + i, crosses)))
+    for i in range(1, 4):
+        greet((row_mate(i), k))
+    for load in loads:
+        load.wait()
 
     for x in range(2):
         flag = iblank[x]
@@ -140,10 +164,8 @@
             low_out[x, v] = cells[0:2]
             high_out[x, v] = cells[14:16]
 
-    pl.semaphore_wait(barrier, canals - 1 + crosses - 1)
-
-    c_next, c_last = lax.rem(c + 1, canals), lax.rem(c + canals - 1, canals)
-    k_next, k_last = lax.rem(k + 1, crosses), lax.rem(k + crosses - 1, crosses)
+    pl.semaphore_wait(barrier, 2 + canals // 4 - 1 + crosses - 1 + 3)
+
     own = known.at[:, :, pl.ds(8, 16), :]
     halo = []
     for number, (source, target, device) in enumerate(
@@ -165,9 +187,13 @@
         copy.start()
         halo.append(copy)
 
+    for i in range(1, 4):
+        pl.semaphore_signal(entered, inc=1, device_id=(row_mate(i), k), device_id_type=MESH)
+
     lane = lax.broadcasted_iota(jnp.int32, TILE, 1)
     sub = lax.broadcasted_iota(jnp.int32, TILE, 0)
     upper_half = sub < 4
+    zero = jnp.zeros(TILE, F32)
 
     def pack(matrices, target):
         for b in range(blocks):
@@ -178,35 +204,6 @@
                 chunk = b * (block // 4) + 2 * n
                 target[chunk] = jnp.where(upper_half, one, pltpu.roll(two, 4, 0))
                 target[chunk + 1] = jnp.where(upper_half, pltpu.roll(one, 4, 0), two)
-
-    pack([jnp.concatenate([weight[x]] * 8, axis=0) for x in range(2)], vertical_weight)
-    v_top = lax.rem(sub, 4) == 0
-    v_lower, v_centre, v_upper = coefficients(speeds, 2, lane // 16, v_top)
-
-    def v_pick(ref, n, step):
-        near, far = ref[n], ref[canals - 1 - n]
-        if step:
-            near = pltpu.roll(near, 8 - step, 0)
-        if step != 2:
-            far = pltpu.roll(far, (step + 6) % 8, 0)
-        return jnp.where(v_top, near, far)
-
-    def v_factor(n, carry):
-        p_one, q_one, p_two, q_two = carry
-        for step in range(4):
-            w = v_pick(vertical_weight, n, step)
-            inverse, multiplier, p_new, q_new = factor(
-                w, v_lower, v_centre, v_upper, p_one, q_one, p_two, q_two
-            )
-            v_inverse[4 * n + step] = inverse
-            v_multiplier[4 * n + step] = multiplier
-            v_p[4 * n + step] = p_new
-            v_q[4 * n + step] = q_new
-            p_one, q_one, p_two, q_two = p_new, q_new, p_one, q_one
-        return p_one, q_one, p_two, q_two
-
-    zero = jnp.zeros(TILE, F32)
-    lax.fori_loop(0, half, v_factor, (zero, zero, zero, zero))
 
     for copy in halo:
         copy.wait()
@@ -268,6 +265,29 @@
         part = ref.at[pl.ds(0, count)]
         pltpu.make_async_copy(part, part, sem).wait()
 
+    def retreat(p_rows, q_rows, g_rows, total, span, x_one, x_two, finish):
+        def block(base, length, x_one, x_two):
+            for i in range(length - 1, -1, -1):
+                n = base + i
+                solved = (g_rows[n] - q_rows[n] * x_two) - p_rows[n] * x_one
+                g_rows[n] = solved
+                x_one, x_two = solved, x_one
+            return x_one, x_two
+
+        start = total - span
+        state = block(start, span - 1, x_one, x_two)
+        finish(start)
+
+        def more(i, state):
+            base = total - span * (i + 2)
+            state = block(base, span, *state)
+            finish(base)
+            return state
+
+        lax.fori_loop(0, total // span - 1, more, state)
+
+    pl.semaphore_wait(entered, 3)
+
     def send_canal(i, carry):
         for sign in (1, -1):
             other = lax.rem(c + sign * (half - i) + canals, canals)
@@ -278,6 +298,35 @@
     send_tile(send_one.at[opposite], recv_one.at[c], (opposite, k), 0)
     lax.fori_loop(1, half, send_canal, 0)
     pltpu.make_async_copy(send_one.at[c], recv_one.at[c], recv_sems.at[0]).start()
+    pack([jnp.concatenate([weight[x]] * 8, axis=0) for x in range(2)], vertical_weight)
+    v_top = lax.rem(sub, 4) == 0
+    v_lower, v_centre, v_upper = coefficients(speeds, 2, lane // 16, v_top)
+
+    def v_pick(ref, n, step):
+        near, far = ref[n], ref[canals - 1 - n]
+        if step:
+            near = pltpu.roll(near, 8 - step, 0)
+        if step != 2:
+            far = pltpu.roll(far, (step + 6) % 8, 0)
+        return jnp.where(v_top, near, far)
+
+    def v_factor(m, carry):
+        p_one, q_one, p_two, q_two = carry
+        for part in range(8):
+            n, step = 2 * m + part // 4, part % 4
+            w = v_pick(vertical_weight, n, step)
+            inverse, multiplier, p_new, q_new = factor(
+                w, v_lower, v_centre, v_upper, p_one, q_one, p_two, q_two
+            )
+            v_inverse[4 * n + step] = inverse
+            v_multiplier[4 * n + step] = multiplier
+            v_p[4 * n + step] = p_new
+            v_q[4 * n + step] = q_new
+            p_one, q_one, p_two, q_two = p_new, q_new, p_one, q_one
+        return p_one, q_one, p_two, q_two
+
+    lax.fori_loop(0, half // 2, v_factor, (zero, zero, zero, zero))
+
     wait_for(recv_one, canals, recv_sems.at[0])
 
     c_lower, c_centre, c_upper = coefficients(speeds, 0, lane // 16, upper_half)
@@ -289,24 +338,26 @@
         w += pltpu.roll(w, 32, 1)
         return w + pltpu.roll(w, 64, 1)
 
-    def c_forward(n, carry):
+    def c_forward(i, carry):
         g_one, p_one, q_one, g_two, p_two, q_two = carry
-        near, far = recv_one[n], recv_one[canals - 1 - n]
-        outer = jnp.where(upper_half, near, far)
-        inner = pltpu.roll(jnp.where(upper_half, far, near), 4, 0)
-        for step, source in enumerate((outer, inner)):
-            w = widen(source)
-            inverse, multiplier, p_new, q_new = factor(
-                w, c_lower, c_centre, c_upper, p_one, q_one, p_two, q_two
-            )
-            g_new = (source * inverse - q_new * g_two) - multiplier * g_one
-            work_g[2 * n + step] = g_new
-            work_p[2 * n + step] = p_new
-            work_q[2 * n + step] = q_new
-            g_one, p_one, q_one, g_two, p_two, q_two = g_new, p_new, q_new, g_one, p_one, q_one
+        for m in range(8):
+            n = 8 * i + m
+            near, far = recv_one[n], recv_one[canals - 1 - n]
+            outer = jnp.where(upper_half, near, far)
+            inner = pltpu.roll(jnp.where(upper_half, far, near), 4, 0)
+            for step, source in enumerate((outer, inner)):
+                w = widen(source)
+                inverse, multiplier, p_new, q_new = factor(
+                    w, c_lower, c_centre, c_upper, p_one, q_one, p_two, q_two
+                )
+                g_new = (source * inverse - q_new * g_two) - multiplier * g_one
+                work_g[2 * n + step] = g_new
+                work_p[2 * n + step] = p_new
+                work_q[2 * n + step] = q_new
+                g_one, p_one, q_one, g_two, p_two, q_two = g_new, p_new, q_new, g_one, p_one, q_one
         return g_one, p_one, q_one, g_two, p_two, q_two
 
-    g_one, p_one, q_one, g_two, p_two, q_two = lax.fori_loop(0, half, c_forward, (zero,) * 6)
+    g_one, p_one, q_one, g_two, p_two, q_two = lax.fori_loop(0, half // 8, c_forward, (zero,) * 6)
 
     def c_swap(a):
         return pltpu.roll(a, 4, 0)
@@ -314,26 +365,18 @@
     x_one = join(c_swap, g_one, g_two, p_one, q_one, p_two, q_two)
     work_g[canals - 1] = x_one
 
-    def c_back(i, carry):
-        x_one, x_two = carry
-        n = canals - 2 - i
-        solved = (work_g[n] - work_q[n] * x_two) - work_p[n] * x_one
-        work_g[n] = solved
-        return solved, x_one
-
-    lax.fori_loop(0, canals - 1, c_back, (x_one, c_swap(x_one)))
-
-    def c_restore(n, carry):
-        outer, inner = work_g[2 * n], pltpu.roll(work_g[2 * n + 1], 4, 0)
-        for pair, tile in (
-            (n, jnp.where(upper_half, outer, inner)),
-            (canals - 1 - n, jnp.where(upper_half, inner, outer)),
-        ):
-            group, place = partner_of(pair, crosses)
-            send_two[group * places + place] = jnp.where(is_weight, recv_one[pair], tile)
-        return carry
-
-    lax.fori_loop(0, half, c_restore, 0)
+    def c_restore(start):
+        for m in range(8):
+            n = start // 2 + m
+            outer, inner = work_g[start + 2 * m], pltpu.roll(work_g[start + 2 * m + 1], 4, 0)
+            for pair, tile in (
+                (n, jnp.where(upper_half, outer, inner)),
+                (canals - 1 - n, jnp.where(upper_half, inner, outer)),
+            ):
+                group, place = partner_of(pair, c, crosses)
+                send_two[group * places + place] = jnp.where(is_weight, recv_one[pair], tile)
+
+    retreat(work_p, work_q, work_g, canals, 16, x_one, c_swap(x_one), c_restore)
 
     def group_of(ref, position):
         return ref.at[pl.ds(position * places, places)]
@@ -385,57 +428,53 @@
     x_one = join(x_swap, g_one, g_two, p_one, q_one, p_two, q_two)
     work_g[16 * count - 1] = x_one
 
-    def x_back(i, carry):
-        x_one, x_two = carry
-        n = 16 * count - 2 - i
-        solved = (work_g[n] - work_q[n] * x_two) - work_p[n] * x_one
-        work_g[n] = solved
-        return solved, x_one
-
-    lax.fori_loop(0, 16 * count - 1, x_back, (x_one, x_swap(x_one)))
-
-    for pair in range(count):
+    def send_home(pair):
+        def one(i, carry):
+            place = lax.rem(i + c, places)
+            target = pair_of(k, c, place, crosses)
+            for other in (pair, crosses - 1 - pair):
+                source = send_three.at[other * places + place]
+                itself = jnp.logical_and(target == c, other == k)
+
+                @pl.when(itself)
+                def keep():
+                    pltpu.make_async_copy(source, recv_three.at[c], recv_sems.at[2]).start()
+
+                @pl.when(jnp.logical_not(itself))
+                def send():
+                    send_tile(source, recv_three.at[c], (target, other), 2)
+
+            return carry
+
+        lax.fori_loop(0, places, one, 0)
+
+    def x_restore(start):
+        pair = start // 16
         for y in range(16):
             turned[pair, pl.ds(y, 8, stride=16), :] = jnp.where(
-                x_top, work_g[16 * pair + y], work_g[16 * pair + 15 - y]
+                x_top, work_g[start + y], work_g[start + 15 - y]
             )
         back = turned[pair].T
-        send_three[pair * places : (pair + 1) * places] = back[:lines].reshape(places, 8, 128)
-        other = crosses - 1 - pair
-        send_three[other * places : (other + 1) * places] = back[lines:].reshape(places, 8, 128)
-
-    def send_home(i, carry):
-        place, other = i // crosses, lax.rem(i, crosses)
-        place = lax.rem(place + c, places)
-        other = lax.rem(other + k, crosses)
-        target = pair_of(k, place, crosses)
-        source = send_three.at[other * places + place]
-        itself = jnp.logical_and(target == c, other == k)
-
-        @pl.when(itself)
-        def keep():
-            pltpu.make_async_copy(source, recv_three.at[c], recv_sems.at[2]).start()
-
-        @pl.when(jnp.logical_not(itself))
-        def send():
-            send_tile(source, recv_three.at[c], (target, other), 2)
-
-        return carry
-
-    lax.fori_loop(0, canals, send_home, 0)
+        for block in range(places):
+            at = 8 * block
+            send_three[pair * places + block] = back[at : at + 8]
+            send_three[(crosses - 1 - pair) * places + block] = back[lines + at : lines + at + 8]
+        send_home(pair)
+
+    retreat(work_p, work_q, work_g, 16 * count, 16, x_one, x_swap(x_one), x_restore)
     wait_for(recv_three, canals, recv_sems.at[2])
 
-    def v_forward(n, carry):
+    def v_forward(m, carry):
         g_one, g_two = carry
-        for step in range(4):
-            i = 4 * n + step
-            source = v_pick(recv_three, n, step)
+        for step in range(16):
+            i = 16 * m + step
+            source = v_pick(recv_three, 4 * m + step // 4, step % 4)
             g_new = (source * v_inverse[i] - v_q[i] * g_two) - v_multiplier[i] * g_one
             v_g[i] = g_new
             g_one, g_two = g_new, g_one
         return g_one, g_two
 
-    g_one, g_two = lax.fori_loop(0, half, v_forward, (zero, zero))
+    g_one, g_two = lax.fori_loop(0, half // 4, v_forward, (zero, zero))
 
     def v_swap(a):
         return jnp.where(v_top, pltpu.roll(a, 7, 0), pltpu.roll(a, 1, 0))
@@ -444,18 +483,9 @@
     x_one = join(v_swap, g_one, g_two, v_p[last], v_q[last], v_p[last - 1], v_q[last - 1])
     v_g[last] = x_one
 
-    def v_back(i, carry):
-        x_one, x_two = carry
-        n = last - 1 - i
-        solved = (v_g[n] - v_q[n] * x_two) - v_p[n] * x_one
-        v_g[n] = solved
-        return solved, x_one
-
-    lax.fori_loop(0, last, v_back, (x_one, v_swap(x_one)))
-
     place_of = lax.rem(sub, 4)
 
-    def v_restore(n, carry):
+    def v_chunk(n):
         near, far = [], []
         for part in range(2):
             base = 8 * n + 4 * part
@@ -478,9 +508,12 @@
         for start, (one, two) in ((at, near), (end, far)):
             upright[0, pl.ds(start, 8), :] = jnp.where(upper_half, one, pltpu.roll(two, 4, 0))
             upright[1, pl.ds(start, 8), :] = jnp.where(upper_half, pltpu.roll(one, 4, 0), two)
-        return carry
-
-    lax.fori_loop(0, half // 2, v_restore, 0)
+
+    def v_restore(start):
+        v_chunk(start // 8)
+        v_chunk(start // 8 + 1)
+
+    retreat(v_p, v_q, v_g, 2 * canals, 16, x_one, v_swap(x_one), v_restore)
 
     for x in range(2):
         for b in range(blocks):
@@ -493,7 +526,7 @@
 
     wait_for(send_one, canals - 1, send_sems.at[0])
     wait_for(send_two, canals - places, send_sems.at[1])
-    mine, unused = partner_of(c, crosses)
+    mine, unused = partner_of(c, c, crosses)
 
     @pl.when(mine == k)
     def sent_fewer():
@@ -512,7 +545,7 @@
 
     def shards(conserved, iblank, step_scale, speeds, left_vectors, right_vectors):
         vmem = pl.BlockSpec(memory_space=pltpu.VMEM)
-        smem = pl.BlockSpec(memory_space=pltpu.SMEM)
+        anywhere = pl.BlockSpec(memory_space=pl.ANY)
 
         def held(*shape):
             return pltpu.VMEM(shape, F32)
@@ -520,9 +553,15 @@
         return pl.pallas_call(
             functools.partial(kernel, canals, crosses),
             out_shape=jax.ShapeDtypeStruct(cells, F32),
-            in_specs=[vmem, vmem, vmem, smem, smem, smem],
+            in_specs=[anywhere] * 6,
             out_specs=vmem,
             scratch_shapes=[
+                held(*cells),
+                pltpu.VMEM((2, 16, depth), jnp.int32),
+                held(2, 16, depth),
+                pltpu.SMEM((3, NVAR), F32),
+                pltpu.SMEM((NVAR, NVAR), F32),
+                pltpu.SMEM((NVAR, NVAR), F32),
                 held(2, NVAR, 32, depth),
                 held(2, 16, depth),
                 held(2, NVAR, 2, depth),
@@ -549,13 +588,15 @@
                 held(max(canals, 8 * crosses), *TILE),
                 held(max(canals, 8 * crosses), *TILE),
                 held(2 * canals, *TILE),
+                pltpu.SemaphoreType.DMA((6,)),
                 pltpu.SemaphoreType.DMA((4,)),
                 pltpu.SemaphoreType.DMA((4,)),
                 pltpu.SemaphoreType.DMA((3,)),
                 pltpu.SemaphoreType.DMA((3,)),
+                pltpu.SemaphoreType.REGULAR,
             ],
             compiler_params=pltpu.CompilerParams(
-                collective_id=0, has_side_effects=True, vmem_limit_bytes=32 * 1024 * 1024
+                collective_id=0, has_side_effects=True, vmem_limit_bytes=60 * 1024 * 1024
             ),
         )(conserved, iblank, step_scale, speeds, left_vectors, right_vectors)
 

time: 83.4 us -> 67.1 us (0.80)
  Pallas kernels: 77.8 us -> 65 us
  local copies, waits for them, and re-layouts: 5.2 us -> 1.64 us
    pallas_call x1, Pallas kernels: 77.8 us -> 65 us  [shards(): pl.pallas_call(functools.partial(kernel, canals, crosses), out_shape=jax....]
    unnamed x13 -> x1, local copies, waits for them, and re-layouts: 5.2 us -> 1.64 us
where the time goes in v1:
time: 67.1 us; the launch traced here: 66.6 us
  Pallas kernels  65 us (97%)
  local copies, waits for them, and re-layouts  1.64 us (2%)
    pallas_call x1, Pallas kernels, shards(): pl.pallas_call(functools.partial(kernel, canals, crosses), out_shape=jax....  65 us
    unnamed x1, local copies, waits for them, and re-layouts  1.64 us

profile of v1, /device:TPU:1, one launch (start us, length us, event | category | flops | bytes accessed | tf_op | source)
XLA Modules:
  0.0 66.6 jit_solution(9502195688787384384)
XLA Ops:
  0.0 65.0 %shard_map.64 = f32[2,7,16,256]{3,2,1,0:T(8,128)} custom-call(f32[2,7,16,256]{3,2,1,0:T(8,128)} %conserved_hbm.1, s32[2,16,256]{2,1,0:T(8,128)} %iblank_hbm.1, f32[2,16,256]{2,1,0:T(8,128)} %step_scale_hbm.1, f32[3,7]{1,0:T(4,128)} %speeds_hbm.1, f32[7,7]{1,0:T(8,128)} %left_hbm.1, f32[7,7]{1,0:T(8,128)} %right_hbm.1), custom_call_target="tpu_custom_call" | custom-call | tf_op jit(solution)/shard_map/pallas_call | solution.py:553
  65.0 1.6 %copy.8 = f32[2,7,16,256]{3,2,1,0:T(8,128)} copy(f32[2,7,16,256]{3,2,1,0:T(8,128)} %shard_map.64) | data formatting | bytes 458752

commit v2 on v1

--- a/solution.py
+++ b/solution.py
@@ -84,6 +84,7 @@
     high_in,
     before,
     after,
+    partial,
     rows,
     send_one,
     recv_one,
@@ -114,6 +115,7 @@
     blocks = depth // block
     places = canals // crosses
     half = canals // 2
+    per = canals // blocks
     c = lax.axis_index("canal")
     k = lax.axis_index("cross")
 
@@ -166,16 +168,16 @@
 
     pl.semaphore_wait(barrier, 2 + canals // 4 - 1 + crosses - 1 + 3)
 
-    own = known.at[:, :, pl.ds(8, 16), :]
+    def lanes(ref, b):
+        return ref.at[:, :, :, pl.ds(b * block, block)]
+
+    transfers = [(high_out, low_in, (c, k_next)), (low_out, high_in, (c, k_last))]
+    for b in range(blocks):
+        own = known.at[:, :, pl.ds(8, 16), pl.ds(b * block, block)]
+        transfers.append((own, lanes(before, b), (c_next, k)))
+        transfers.append((own, lanes(after, b), (c_last, k)))
     halo = []
-    for number, (source, target, device) in enumerate(
-        (
-            (own, before, (c_next, k)),
-            (own, after, (c_last, k)),
-            (high_out, low_in, (c, k_next)),
-            (low_out, high_in, (c, k_last)),
-        )
-    ):
+    for number, (source, target, device) in enumerate(transfers):
         copy = pltpu.make_async_remote_copy(
             src_ref=source,
             dst_ref=target,
@@ -195,61 +197,36 @@
     upper_half = sub < 4
     zero = jnp.zeros(TILE, F32)
 
-    def pack(matrices, target):
-        for b in range(blocks):
-            first = matrices[0][:, b * block : (b + 1) * block].T
-            second = matrices[1][:, b * block : (b + 1) * block].T
-            for n in range(block // 8):
-                one, two = first[8 * n : 8 * n + 8], second[8 * n : 8 * n + 8]
-                chunk = b * (block // 4) + 2 * n
-                target[chunk] = jnp.where(upper_half, one, pltpu.roll(two, 4, 0))
-                target[chunk + 1] = jnp.where(upper_half, pltpu.roll(one, 4, 0), two)
-
-    for copy in halo:
-        copy.wait()
-
+    def pack(matrices, target, b):
+        first, second = matrices[0].T, matrices[1].T
+        for n in range(block // 8):
+            one, two = first[8 * n : 8 * n + 8], second[8 * n : 8 * n + 8]
+            chunk = b * per + 2 * n
+            target[chunk] = jnp.where(upper_half, one, pltpu.roll(two, 4, 0))
+            target[chunk + 1] = jnp.where(upper_half, pltpu.roll(one, 4, 0), two)
+
+    halo[0].wait_recv()
+    halo[1].wait_recv()
     has_last, has_next = c > 0, c < canals - 1
     low_mask, high_mask = k > 0, k < crosses - 1
     zi = lax.broadcasted_iota(jnp.int32, (16, depth), 1)
     for x in range(2):
-        fluxes = []
         for v in range(NVAR):
             known[x, v, 6:8, :] = jnp.where(low_mask, low_in[x, v], 0.0)
             known[x, v, 24:26, :] = jnp.where(high_mask, high_in[x, v], 0.0)
             here = known[x, v, 8:24, :]
-            if x == 0:
-                minus_one = jnp.where(has_last, before[1, v], 0.0)
-                minus_two = jnp.where(has_last, before[0, v], 0.0)
-                plus_one = known[1, v, 8:24, :]
-                plus_two = jnp.where(has_next, after[0, v], 0.0)
-            else:
-                minus_one = known[0, v, 8:24, :]
-                minus_two = jnp.where(has_last, before[1, v], 0.0)
-                plus_one = jnp.where(has_next, after[0, v], 0.0)
-                plus_two = jnp.where(has_next, after[1, v], 0.0)
-            canal_half = 0.5 * speeds[0, v]
-            flux = (canal_half - 0.125) * plus_one - (canal_half + 0.125) * minus_one
-            outer = plus_two + minus_two
-            cross_half = 0.5 * speeds[1, v]
-            flux += (cross_half - 0.125) * known[x, v, 9:25, :]
-            flux -= (cross_half + 0.125) * known[x, v, 7:23, :]
-            outer += known[x, v, 10:26, :] + known[x, v, 6:22, :]
             z_half = 0.5 * speeds[2, v]
             up_one = jnp.where(zi < depth - 1, pltpu.roll(here, depth - 1, 1), 0.0)
             up_two = jnp.where(zi < depth - 2, pltpu.roll(here, depth - 2, 1), 0.0)
             down_one = jnp.where(zi >= 1, pltpu.roll(here, 1, 1), 0.0)
             down_two = jnp.where(zi >= 2, pltpu.roll(here, 2, 1), 0.0)
-            flux += (z_half - 0.125) * up_one - (z_half + 0.125) * down_one
-            outer += up_two + down_two
-            fluxes.append(flux + (outer + 18.0 * here) * (1.0 / 32.0))
-        scale = weight[x]
-        for v in range(NVAR):
-            mixed = left[v, 0] * fluxes[0]
-            for u in range(1, NVAR):
-                mixed += left[v, u] * fluxes[u]
-            rows[x, 16 * v : 16 * v + 16, :] = -(scale * mixed)
-        rows[x, 112:128, :] = scale
-    pack([rows[0], rows[1]], send_one)
+            flux = (z_half - 0.125) * up_one - (z_half + 0.125) * down_one
+            outer = up_two + down_two
+            cross_half = 0.5 * speeds[1, v]
+            flux += (cross_half - 0.125) * known[x, v, 9:25, :]
+            flux -= (cross_half + 0.125) * known[x, v, 7:23, :]
+            outer += known[x, v, 10:26, :] + known[x, v, 6:22, :]
+            partial[x, v] = flux + (outer + 18.0 * here) * (1.0 / 32.0)
 
     def send_tile(source, target, device, number):
         pltpu.make_async_remote_copy(
@@ -287,18 +264,63 @@
         lax.fori_loop(0, total // span - 1, more, state)
 
     pl.semaphore_wait(entered, 3)
-
-    def send_canal(i, carry):
-        for sign in (1, -1):
-            other = lax.rem(c + sign * (half - i) + canals, canals)
-            send_tile(send_one.at[other], recv_one.at[c], (other, k), 0)
-        return carry
-
-    opposite = lax.rem(c + half, canals)
-    send_tile(send_one.at[opposite], recv_one.at[c], (opposite, k), 0)
-    lax.fori_loop(1, half, send_canal, 0)
-    pltpu.make_async_copy(send_one.at[c], recv_one.at[c], recv_sems.at[0]).start()
-    pack([jnp.concatenate([weight[x]] * 8, axis=0) for x in range(2)], vertical_weight)
+    middle = c // blocks
+
+    def to_canal(b, m):
+        other = blocks * m + b
+        send_tile(send_one.at[b * per + m], recv_one.at[c], (other, k), 0)
+
+    for b in range(blocks):
+        halo[2 + 2 * b].wait_recv()
+        halo[3 + 2 * b].wait_recv()
+        here = slice(b * block, (b + 1) * block)
+        for x in range(2):
+            fluxes = []
+            for v in range(NVAR):
+                if x == 0:
+                    minus_one = jnp.where(has_last, before[1, v, :, here], 0.0)
+                    minus_two = jnp.where(has_last, before[0, v, :, here], 0.0)
+                    plus_one = known[1, v, 8:24, here]
+                    plus_two = jnp.where(has_next, after[0, v, :, here], 0.0)
+                else:
+                    minus_one = known[0, v, 8:24, here]
+                    minus_two = jnp.where(has_last, before[1, v, :, here], 0.0)
+                    plus_one = jnp.where(has_next, after[0, v, :, here], 0.0)
+                    plus_two = jnp.where(has_next, after[1, v, :, here], 0.0)
+                canal_half = 0.5 * speeds[0, v]
+                flux = (canal_half - 0.125) * plus_one - (canal_half + 0.125) * minus_one
+                fluxes.append(partial[x, v, :, here] + (flux + (plus_two + minus_two) * (1.0 / 32.0)))
+            scale = weight[x, :, here]
+            for v in range(NVAR):
+                mixed = left[v, 0] * fluxes[0]
+                for u in range(1, NVAR):
+                    mixed += left[v, u] * fluxes[u]
+                rows[x, 16 * v : 16 * v + 16, here] = -(scale * mixed)
+            rows[x, 112:128, here] = scale
+        pack([rows[x, :, here] for x in range(2)], send_one, b)
+
+        def send_canal(i, carry):
+            for sign in (1, -1):
+                to_canal(b, lax.rem(middle + sign * (per // 2 - i) + per, per))
+            return carry
+
+        to_canal(b, lax.rem(middle + per // 2, per))
+        lax.fori_loop(1, per // 2, send_canal, 0)
+        mine_now = lax.rem(c, blocks) == b
+
+        @pl.when(mine_now)
+        def keep_own():
+            pltpu.make_async_copy(
+                send_one.at[b * per + middle], recv_one.at[c], recv_sems.at[0]
+            ).start()
+
+        @pl.when(jnp.logical_not(mine_now))
+        def send_near():
+            to_canal(b, middle)
+
+    for b in range(blocks):
+        here = slice(b * block, (b + 1) * block)
+        pack([jnp.concatenate([weight[x, :, here]] * 8, axis=0) for x in range(2)], vertical_weight, b)
     v_top = lax.rem(sub, 4) == 0
     v_lower, v_centre, v_upper = coefficients(speeds, 2, lane // 16, v_top)
 
@@ -428,6 +450,8 @@
     x_one = join(x_swap, g_one, g_two, p_one, q_one, p_two, q_two)
     work_g[16 * count - 1] = x_one
 
+    chunk_here = c // blocks + per * lax.rem(c, blocks)
+
     def send_home(pair):
         def one(i, carry):
             place = lax.rem(i + c, places)
@@ -438,11 +462,11 @@
 
                 @pl.when(itself)
                 def keep():
-                    pltpu.make_async_copy(source, recv_three.at[c], recv_sems.at[2]).start()
+                    pltpu.make_async_copy(source, recv_three.at[chunk_here], recv_sems.at[2]).start()
 
                 @pl.when(jnp.logical_not(itself))
                 def send():
-                    send_tile(source, recv_three.at[c], (target, other), 2)
+                    send_tile(source, recv_three.at[chunk_here], (target, other), 2)
 
             return carry
 
@@ -524,6 +548,8 @@
                     mixed += right[v, u] * third[16 * u : 16 * u + 16]
                 update[x, v, :, b * block : (b + 1) * block] = mixed
 
+    for copy in halo:
+        copy.wait_send()
     wait_for(send_one, canals - 1, send_sems.at[0])
     wait_for(send_two, canals - places, send_sems.at[1])
     mine, unused = partner_of(c, c, crosses)
@@ -542,6 +568,7 @@
     depth = 4 * canals
     cells = (2, NVAR, 16, depth)
     tiles = (canals,) + TILE
+    transfers = 2 + 2 * (depth // min(depth, 128))
 
     def shards(conserved, iblank, step_scale, speeds, left_vectors, right_vectors):
         vmem = pl.BlockSpec(memory_space=pltpu.VMEM)
@@ -568,6 +595,7 @@
                 held(2, NVAR, 2, depth),
                 held(2, NVAR, 2, depth),
                 held(2, NVAR, 2, depth),
+                held(*cells),
                 held(*cells),
                 held(*cells),
                 held(2, 128, depth),
@@ -589,8 +617,8 @@
                 held(max(canals, 8 * crosses), *TILE),
                 held(2 * canals, *TILE),
                 pltpu.SemaphoreType.DMA((6,)),
-                pltpu.SemaphoreType.DMA((4,)),
-                pltpu.SemaphoreType.DMA((4,)),
+                pltpu.SemaphoreType.DMA((transfers,)),
+                pltpu.SemaphoreType.DMA((transfers,)),
                 pltpu.SemaphoreType.DMA((3,)),
                 pltpu.SemaphoreType.DMA((3,)),
                 pltpu.SemaphoreType.REGULAR,

time: 67.1 us -> 66.4 us (0.990)
  no operation moved by 1% of the time
where the time goes in v2:
time: 66.4 us; the launch traced here: 66.2 us
  Pallas kernels  64.5 us (97%)
  local copies, waits for them, and re-layouts  1.64 us (2%)
    pallas_call x1, Pallas kernels, shards(): pl.pallas_call(functools.partial(kernel, canals, crosses), out_shape=jax....  64.5 us
    unnamed x1, local copies, waits for them, and re-layouts  1.64 us

profile of v2, /device:TPU:1, one launch (start us, length us, event | category | flops | bytes accessed | tf_op | source)
XLA Modules:
  0.0 66.2 jit_solution(8320955688894025655)
XLA Ops:
  0.0 64.5 %shard_map.64 = f32[2,7,16,256]{3,2,1,0:T(8,128)} custom-call(f32[2,7,16,256]{3,2,1,0:T(8,128)} %conserved_hbm.1, s32[2,16,256]{2,1,0:T(8,128)} %iblank_hbm.1, f32[2,16,256]{2,1,0:T(8,128)} %step_scale_hbm.1, f32[3,7]{1,0:T(4,128)} %speeds_hbm.1, f32[7,7]{1,0:T(8,128)} %left_hbm.1, f32[7,7]{1,0:T(8,128)} %right_hbm.1), custom_call_target="tpu_custom_call" | custom-call | tf_op jit(solution)/shard_map/pallas_call | solution.py:580
  64.5 1.6 %copy.8 = f32[2,7,16,256]{3,2,1,0:T(8,128)} copy(f32[2,7,16,256]{3,2,1,0:T(8,128)} %shard_map.64) | data formatting | bytes 458752

commit v3 on v2

--- a/solution.py
+++ b/solution.py
@@ -29,7 +29,7 @@
     damping = 0.25 * w
     reduced = w * (0.25 * p_two - lower)
     pivot = (1.0 + centre * w + damping * q_two) - reduced * p_one
-    inverse = 1.0 / pivot
+    inverse = pl.reciprocal(pivot, approx=True)
     q_new = -damping * inverse
     p_new = -(upper * w + reduced * q_one) * inverse
     return inverse, reduced * inverse, p_new, q_new
@@ -93,6 +93,7 @@
     turned,
     send_three,
     recv_three,
+    home,
     vertical_weight,
     upright,
     v_inverse,
@@ -472,6 +473,15 @@
 
         lax.fori_loop(0, places, one, 0)
 
+    diagonal = lane // 16 == sub
+
+    def fold(tile):
+        last_row = jnp.where(diagonal, jnp.broadcast_to(tile[7:8], TILE), 0.0)
+        last_row += pltpu.roll(last_row, 16, 1)
+        last_row += pltpu.roll(last_row, 32, 1)
+        last_row += pltpu.roll(last_row, 64, 1)
+        return jnp.where(is_weight, last_row, tile)[0:7]
+
     def x_restore(start):
         pair = start // 16
         for y in range(16):
@@ -481,18 +491,31 @@
         back = turned[pair].T
         for block in range(places):
             at = 8 * block
-            send_three[pair * places + block] = back[at : at + 8]
-            send_three[(crosses - 1 - pair) * places + block] = back[lines + at : lines + at + 8]
+            send_three[pair * places + block] = fold(back[at : at + 8])
+            send_three[(crosses - 1 - pair) * places + block] = fold(back[lines + at : lines + at + 8])
         send_home(pair)
 
     retreat(work_p, work_q, work_g, 16 * count, 16, x_one, x_swap(x_one), x_restore)
     wait_for(recv_three, canals, recv_sems.at[2])
+
+    def unfold(i, carry):
+        for m in range(8):
+            n = 8 * i + m
+            home[n, 0:7] = recv_three[n]
+            free = jnp.where(is_weight[0:7], recv_three[n], 0.0)
+            free += pltpu.roll(free, 16, 1)
+            free += pltpu.roll(free, 32, 1)
+            free += pltpu.roll(free, 64, 1)
+            home[n, 7:8] = jnp.sum(jnp.where(diagonal[0:7], free, 0.0), axis=0, keepdims=True)
+        return carry
+
+    lax.fori_loop(0, canals // 8, unfold, 0)
 
     def v_forward(m, carry):
         g_one, g_two = carry
         for step in range(16):
             i = 16 * m + step
-            source = v_pick(recv_three, 4 * m + step // 4, step % 4)
+            source = v_pick(home, 4 * m + step // 4, step % 4)
             g_new = (source * v_inverse[i] - v_q[i] * g_two) - v_multiplier[i] * g_one
             v_g[i] = g_new
             g_one, g_two = g_new, g_one
@@ -604,7 +627,8 @@
                 held(*tiles),
                 held(*tiles),
                 held(crosses // 2, 128, 16 * (canals // crosses)),
-                held(*tiles),
+                held(canals, 7, 128),
+                held(canals, 7, 128),
                 held(*tiles),
                 held(*tiles),
                 held(2, depth, 128),

time: 66.4 us -> 67.2 us (1.012)
  no operation moved by 1% of the time
where the time goes in v3:
time: 67.2 us; the launch traced here: 66.5 us
  Pallas kernels  64.8 us (96%)
  local copies, waits for them, and re-layouts  1.64 us (2%)
    pallas_call x1, Pallas kernels, shards(): pl.pallas_call(functools.partial(kernel, canals, crosses), out_shape=jax....  64.8 us
    unnamed x1, local copies, waits for them, and re-layouts  1.64 us

profile of v3, /device:TPU:1, one launch (start us, length us, event | category | flops | bytes accessed | tf_op | source)
XLA Modules:
  0.0 66.5 jit_solution(8888608506374741344)
XLA Ops:
  0.0 64.8 %shard_map.64 = f32[2,7,16,256]{3,2,1,0:T(8,128)} custom-call(f32[2,7,16,256]{3,2,1,0:T(8,128)} %conserved_hbm.1, s32[2,16,256]{2,1,0:T(8,128)} %iblank_hbm.1, f32[2,16,256]{2,1,0:T(8,128)} %step_scale_hbm.1, f32[3,7]{1,0:T(4,128)} %speeds_hbm.1, f32[7,7]{1,0:T(8,128)} %left_hbm.1, f32[7,7]{1,0:T(8,128)} %right_hbm.1), custom_call_target="tpu_custom_call" | custom-call | tf_op jit(solution)/shard_map/pallas_call | solution.py:603
  64.8 1.6 %copy.8 = f32[2,7,16,256]{3,2,1,0:T(8,128)} copy(f32[2,7,16,256]{3,2,1,0:T(8,128)} %shard_map.64) | data formatting | bytes 458752

commit v4 on v2

--- a/solution.py
+++ b/solution.py
@@ -95,6 +95,7 @@
     recv_three,
     vertical_weight,
     upright,
+    result,
     v_inverse,
     v_multiplier,
     v_p,
@@ -108,6 +109,7 @@
     halo_recv,
     send_sems,
     recv_sems,
+    out_sems,
     entered,
 ):
     depth = 4 * canals
@@ -539,6 +541,7 @@
 
     retreat(v_p, v_q, v_g, 2 * canals, 16, x_one, v_swap(x_one), v_restore)
 
+    outgoing = []
     for x in range(2):
         for b in range(blocks):
             third = upright[x, b * block : (b + 1) * block, :].T
@@ -546,7 +549,14 @@
                 mixed = right[v, 0] * third[0:16]
                 for u in range(1, NVAR):
                     mixed += right[v, u] * third[16 * u : 16 * u + 16]
-                update[x, v, :, b * block : (b + 1) * block] = mixed
+                result[x, v, :, b * block : (b + 1) * block] = mixed
+            finished = pltpu.make_async_copy(
+                result.at[x, :, :, pl.ds(b * block, block)],
+                update.at[x, :, :, pl.ds(b * block, block)],
+                out_sems.at[x * blocks + b],
+            )
+            finished.start()
+            outgoing.append(finished)
 
     for copy in halo:
         copy.wait_send()
@@ -561,6 +571,9 @@
     @pl.when(mine != k)
     def sent_all():
         wait_for(send_three, canals, send_sems.at[2])
+
+    for finished in outgoing:
+        finished.wait()
 
 
 def solution(mesh):
@@ -571,7 +584,6 @@
     transfers = 2 + 2 * (depth // min(depth, 128))
 
     def shards(conserved, iblank, step_scale, speeds, left_vectors, right_vectors):
-        vmem = pl.BlockSpec(memory_space=pltpu.VMEM)
         anywhere = pl.BlockSpec(memory_space=pl.ANY)
 
         def held(*shape):
@@ -581,7 +593,7 @@
             functools.partial(kernel, canals, crosses),
             out_shape=jax.ShapeDtypeStruct(cells, F32),
             in_specs=[anywhere] * 6,
-            out_specs=vmem,
+            out_specs=anywhere,
             scratch_shapes=[
                 held(*cells),
                 pltpu.VMEM((2, 16, depth), jnp.int32),
@@ -608,6 +620,7 @@
                 held(*tiles),
                 held(*tiles),
                 held(2, depth, 128),
+                held(*cells),
                 held(2 * canals, *TILE),
                 held(2 * canals, *TILE),
                 held(2 * canals, *TILE),
@@ -621,6 +634,7 @@
                 pltpu.SemaphoreType.DMA((transfers,)),
                 pltpu.SemaphoreType.DMA((3,)),
                 pltpu.SemaphoreType.DMA((3,)),
+                pltpu.SemaphoreType.DMA((transfers - 2,)),
                 pltpu.SemaphoreType.REGULAR,
             ],
             compiler_params=pltpu.CompilerParams(

time: 66.4 us -> 66.4 us (level)
  no operation moved by 1% of the time
where the time goes in v4:
time: 66.4 us; the launch traced here: 66.1 us
  Pallas kernels  64.5 us (97%)
  local copies, waits for them, and re-layouts  1.64 us (2%)
    pallas_call x1, Pallas kernels, shards(): pl.pallas_call(functools.partial(kernel, canals, crosses), out_shape=jax....  64.5 us
    unnamed x1, local copies, waits for them, and re-layouts  1.64 us

profile of v4, /device:TPU:1, one launch (start us, length us, event | category | flops | bytes accessed | tf_op | source)
XLA Modules:
  0.0 66.1 jit_solution(15010547628326351086)
XLA Ops:
  0.0 64.5 %shard_map.64 = f32[2,7,16,256]{3,2,1,0:T(8,128)} custom-call(f32[2,7,16,256]{3,2,1,0:T(8,128)} %conserved_hbm.1, s32[2,16,256]{2,1,0:T(8,128)} %iblank_hbm.1, f32[2,16,256]{2,1,0:T(8,128)} %step_scale_hbm.1, f32[3,7]{1,0:T(4,128)} %speeds_hbm.1, f32[7,7]{1,0:T(8,128)} %left_hbm.1, f32[7,7]{1,0:T(8,128)} %right_hbm.1), custom_call_target="tpu_custom_call" | custom-call | tf_op jit(solution)/shard_map/pallas_call | solution.py:592
  64.5 1.6 %copy.8 = f32[2,7,16,256]{3,2,1,0:T(8,128)} copy(f32[2,7,16,256]{3,2,1,0:T(8,128)} %shard_map.64) | data formatting | bytes 458752

commit v5 on v4

--- a/solution.py
+++ b/solution.py
@@ -307,7 +307,7 @@
             return carry
 
         to_canal(b, lax.rem(middle + per // 2, per))
-        lax.fori_loop(1, per // 2, send_canal, 0)
+        lax.fori_loop(1, per // 2, send_canal, 0, unroll=True)
         mine_now = lax.rem(c, blocks) == b
 
         @pl.when(mine_now)
@@ -472,7 +472,7 @@
 
             return carry
 
-        lax.fori_loop(0, places, one, 0)
+        lax.fori_loop(0, places, one, 0, unroll=True)
 
     def x_restore(start):
         pair = start // 16

time: 66.4 us -> 66.3 us (level)
  Pallas kernels: 64.5 us -> 63.7 us
    pallas_call x1, Pallas kernels: 64.5 us -> 63.7 us  [shards(): pl.pallas_call(functools.partial(kernel, canals, crosses), out_shape=jax....]
where the time goes in v5:
time: 66.3 us; the launch traced here: 65.4 us
  Pallas kernels  63.7 us (96%)
  local copies, waits for them, and re-layouts  1.64 us (2%)
    pallas_call x1, Pallas kernels, shards(): pl.pallas_call(functools.partial(kernel, canals, crosses), out_shape=jax....  63.7 us
    unnamed x1, local copies, waits for them, and re-layouts  1.64 us

profile of v5, /device:TPU:1, one launch (start us, length us, event | category | flops | bytes accessed | tf_op | source)
XLA Modules:
  0.0 65.4 jit_solution(6422406725240333477)
XLA Ops:
  0.0 63.7 %shard_map.64 = f32[2,7,16,256]{3,2,1,0:T(8,128)} custom-call(f32[2,7,16,256]{3,2,1,0:T(8,128)} %conserved_hbm.1, s32[2,16,256]{2,1,0:T(8,128)} %iblank_hbm.1, f32[2,16,256]{2,1,0:T(8,128)} %step_scale_hbm.1, f32[3,7]{1,0:T(4,128)} %speeds_hbm.1, f32[7,7]{1,0:T(8,128)} %left_hbm.1, f32[7,7]{1,0:T(8,128)} %right_hbm.1), custom_call_target="tpu_custom_call" | custom-call | tf_op jit(solution)/shard_map/pallas_call | solution.py:592
  63.8 1.6 %copy.8 = f32[2,7,16,256]{3,2,1,0:T(8,128)} copy(f32[2,7,16,256]{3,2,1,0:T(8,128)} %shard_map.64) | data formatting | bytes 458752

commit v6 on v4

--- a/solution.py
+++ b/solution.py
@@ -147,10 +147,10 @@
     def row_mate(i):
         return 4 * (c // 4) + lax.rem(c + i, 4)
 
+    for i in sorted(range(1, canals // 4), key=lambda i: abs(i - canals // 8)):
+        greet((lax.rem(c + 4 * i, canals), k))
     greet((c_next, k))
     greet((c_last, k))
-    for i in range(1, canals // 4):
-        greet((lax.rem(c + 4 * i, canals), k))
     for i in range(1, crosses):
         greet((c, lax.rem(k + i, crosses)))
     for i in range(1, 4):

time: 66.4 us -> 66.5 us (level)
  no operation moved by 1% of the time
where the time goes in v6:
time: 66.5 us; the launch traced here: 65.6 us
  Pallas kernels  63.9 us (96%)
  local copies, waits for them, and re-layouts  1.64 us (2%)
    pallas_call x1, Pallas kernels, shards(): pl.pallas_call(functools.partial(kernel, canals, crosses), out_shape=jax....  63.9 us
    unnamed x1, local copies, waits for them, and re-layouts  1.64 us

profile of v6, /device:TPU:1, one launch (start us, length us, event | category | flops | bytes accessed | tf_op | source)
XLA Modules:
  0.0 65.6 jit_solution(6306195081379165572)
XLA Ops:
  0.0 63.9 %shard_map.64 = f32[2,7,16,256]{3,2,1,0:T(8,128)} custom-call(f32[2,7,16,256]{3,2,1,0:T(8,128)} %conserved_hbm.1, s32[2,16,256]{2,1,0:T(8,128)} %iblank_hbm.1, f32[2,16,256]{2,1,0:T(8,128)} %step_scale_hbm.1, f32[3,7]{1,0:T(4,128)} %speeds_hbm.1, f32[7,7]{1,0:T(8,128)} %left_hbm.1, f32[7,7]{1,0:T(8,128)} %right_hbm.1), custom_call_target="tpu_custom_call" | custom-call | tf_op jit(solution)/shard_map/pallas_call | solution.py:592
  63.9 1.6 %copy.8 = f32[2,7,16,256]{3,2,1,0:T(8,128)} copy(f32[2,7,16,256]{3,2,1,0:T(8,128)} %shard_map.64) | data formatting | bytes 458752
